TPU v7x, 128 devices: a whole 4x4x4 slice. The times are simulated.
128 devices in a mesh: gx: 32 (over x, z, core), gy: 4 (over y).
Axes of the slice: x: 4, y: 4, z: 4, core: 2. Of those that a mesh axis runs over, the one named last changes fastest.
Arguments:
- field: float32 [3, 8, 2048, 2048], P(None, None, 'gx', 'gy'), may hold values from -6 to 6
Outputs:
- spectrum: float32 [2, 3, 8, 2048, 2048], P(None, None, None, ('gx', 'gy'))
All inputs are finite; a program needn't handle non-finite values.
Results may differ from a plain program's by a relative error of at most 0.000092.
Values sent between devices are 32-bit elements; how exact they have to be, the bound alone decides.
A program may use at most 128 MiB of HBM per device.

v0:
```python
import math

import jax
import jax.numpy as jnp
from jax import lax
from jax.sharding import PartitionSpec as P

HIGH = lax.Precision.HIGHEST


def swapped(value, axis, apart):
    mask = 2**apart
    pairs = [(source, source ^ mask) for source in range(lax.axis_size(axis))]
    return lax.ppermute(value, axis, pairs)


def reverse_digits(value, digits):
    total = jnp.zeros_like(value)
    for place in range(digits):
        total = total + ((value >> place & 1) << digits - 1 - place)
    return total


def phase_table(rows, cols, length):
    phase = rows[:, None] * cols[None, :] % length
    angle = phase.astype(jnp.float32) * (-2.0 * math.pi / length)
    return (jnp.cos(angle), jnp.sin(angle))


def complex_apply(form, table_re, table_im, data_re, data_im):
    first = jnp.einsum(form, table_re, data_re, precision=HIGH) - jnp.einsum(
        form, table_im, data_im, precision=HIGH
    )
    second = jnp.einsum(form, table_re, data_im, precision=HIGH) + jnp.einsum(
        form, table_im, data_re, precision=HIGH
    )
    return (first, second)


def per_device(field):
    groups = lax.axis_size("gx")
    digits = groups.bit_length() - 1
    device = lax.axis_index("gx")
    comp, planes, cells_x, cells_y = field.shape
    total_x = cells_x * groups
    partner = swapped(field, "gx", digits - 1)
    digit = device >> digits - 1 & 1
    upper = digit == 1
    lower_part = jnp.where(upper, partner, field)
    upper_part = jnp.where(upper, field, partner)
    sign = (1 - 2 * digit).astype(jnp.float32)
    partial_value = jnp.stack([lower_part + sign * upper_part, jnp.zeros_like(field)])
    kappa = digit
    for section in range(1, digits):
        place = digits - 1 - section
        other = swapped(partial_value, "gx", place)
        digit = device >> place & 1
        kappa = kappa + (digit << section)
        angle = kappa.astype(jnp.float32) * (-2.0 * math.pi / 2 ** (section + 1))
        twist_re = jnp.cos(angle)
        twist_im = jnp.sin(angle)
        upper = digit == 1
        lower_part = jnp.where(upper, other, partial_value)
        upper_part = jnp.where(upper, partial_value, other)
        partial_value = jnp.stack(
            [
                lower_part[0] + twist_re * upper_part[0] - twist_im * upper_part[1],
                lower_part[1] + twist_re * upper_part[1] + twist_im * upper_part[0],
            ]
        )
    flipped = reverse_digits(device, digits)
    within = jnp.arange(cells_x, dtype=jnp.int32)
    phase = within * flipped % total_x
    angle = phase.astype(jnp.float32) * (-2.0 * math.pi / total_x)
    twist_re = jnp.cos(angle)[:, None]
    twist_im = jnp.sin(angle)[:, None]
    turned_re = partial_value[0] * twist_re - partial_value[1] * twist_im
    turned_im = partial_value[0] * twist_im + partial_value[1] * twist_re
    table_re, table_im = phase_table(within, within, cells_x)
    done_re, done_im = complex_apply("km,czmy->czky", table_re, table_im, turned_re, turned_im)
    spectrum_x = jnp.stack([done_re, done_im])
    scale = 1.0 / math.sqrt(total_x * cells_y * lax.axis_size("gy"))
    block = lax.all_to_all(spectrum_x, "gy", split_axis=3, concat_axis=4, tiled=True)
    lines = block.shape[4]
    inner = math.gcd(lines, 128)
    outer = lines // inner
    shaped = block.reshape(block.shape[:4] + (outer, inner))
    outer_idx = jnp.arange(outer, dtype=jnp.int32)
    inner_idx = jnp.arange(inner, dtype=jnp.int32)
    outer_re, outer_im = phase_table(outer_idx, outer_idx, outer)
    step_re, step_im = complex_apply("cb,...ba->...ca", outer_re, outer_im, shaped[0], shaped[1])
    cross_re, cross_im = phase_table(outer_idx, inner_idx, lines)
    rot_re = step_re * cross_re - step_im * cross_im
    rot_im = step_re * cross_im + step_im * cross_re
    inner_re, inner_im = phase_table(inner_idx, inner_idx, inner)
    last_re, last_im = complex_apply("ea,...ca->...ec", inner_re, inner_im, rot_re, rot_im)
    result = jnp.stack([last_re, last_im]) * scale
    return result.reshape(block.shape)


def solution(mesh):
    in_specs = (P(None, None, "gx", "gy"),)
    out_specs = P(None, None, None, ("gx", "gy"), None)
    return jax.shard_map(
        per_device, mesh=mesh, in_specs=in_specs, out_specs=out_specs, check_vma=False
    )
```

profile of v0, /device:TPU:3, one launch (start us, length us, event | category | flops | bytes accessed | tf_op | source)
XLA Modules:
  0.0 771.5 jit_solution(7048311023320156620)
XLA Ops:
  1.8 68.9 %collective-permute-done = f32[3,8,64,512]{3,2,1,0:T(8,128)} collective-permute-done((f32[3,8,64,512]{3,2,1,0:T(8,128)}, f32[3,8,64,512]{3,2,1,0:T(8,128)}, u32[]{:S(2)}, u32[]{:S(2)}) %collective-permute-start) | collective-permute-done | bytes 3145760 | tf_op jit(solution)/shard_map/ppermute | solution.py:14
  78.2 135.6 %collective-permute-done.1 = f32[2,3,8,64,512]{4,3,2,1,0:T(8,128)} collective-permute-done((f32[2,3,8,64,512]{4,3,2,1,0:T(8,128)}, f32[2,3,8,64,512]{4,3,2,1,0:T(8,128)}, u32[]{:S(2)}, u32[]{:S(2)}) %collective-permute-start.1) | collective-permute-done | bytes 6291488 | tf_op jit(solution)/shard_map/ppermute | solution.py:14
  213.8 7.8 %broadcast_select_fusion = (f32[2,3,8,64,512]{4,3,2,1,0:T(8,128)S(1)}, f32[2,3,8,64,512]{4,3,2,1,0:T(8,128)}) fusion(f32[2,3,8,64,512]{4,3,2,1,0:T(8,128)} %collective-permute-done.1, pred[]{:T(512)S(6)} %eq.28, f32[1,3,8,64,512]{4,3,2,1,0:T(8,128)S(1)} %add_bitcast_fusion.2), kind=kLoop, calls=%fused_computation.37 | loop fusion | flops 3145728 | bytes 22020096 | tf_op jit(solution)/shard_map/jit(_where)/select_n | solution.py:64
  221.6 4.5 fusion.9
  233.6 133.5 %collective-permute-done.2 = f32[2,3,8,64,512]{4,3,2,1,0:T(8,128)} collective-permute-done((f32[2,3,8,64,512]{4,3,2,1,0:T(8,128)}, f32[2,3,8,64,512]{4,3,2,1,0:T(8,128)}, u32[]{:S(2)}, u32[]{:S(2)}) %collective-permute-start.2) | collective-permute-done | bytes 6291488 | tf_op jit(solution)/shard_map/ppermute | solution.py:14
  367.1 4.6 broadcast_select_fusion.2
  378.4 133.3 %collective-permute-done.3 = f32[2,3,8,64,512]{4,3,2,1,0:T(8,128)} collective-permute-done((f32[2,3,8,64,512]{4,3,2,1,0:T(8,128)}, f32[2,3,8,64,512]{4,3,2,1,0:T(8,128)}, u32[]{:S(2)}, u32[]{:S(2)}) %collective-permute-start.3) | collective-permute-done | bytes 6291488 | tf_op jit(solution)/shard_map/ppermute | solution.py:14
  511.7 4.6 broadcast_select_fusion.4
  526.2 9.9 %collective-permute-done.4 = f32[2,3,8,64,512]{4,3,2,1,0:T(8,128)} collective-permute-done((f32[2,3,8,64,512]{4,3,2,1,0:T(8,128)}, f32[2,3,8,64,512]{4,3,2,1,0:T(8,128)}, u32[]{:S(2)}, u32[]{:S(2)}) %collective-permute-start.4) | collective-permute-done | bytes 6291488 | tf_op jit(solution)/shard_map/ppermute | solution.py:14
  536.1 6.3 broadcast_select_fusion.6
  542.4 4.4 fusion.3
  554.8 4.8 add_bitcast_fusion.1
  565.2 6.4 copy.8
  571.5 5.3 all-to-all-start
  576.9 71.0 %all-to-all-done = f32[2,3,8,64,512]{4,2,1,0,3:T(8,128)} async-done(((f32[2,3,8,64,512]{4,2,1,0,3:T(8,128)}), f32[2,3,8,64,512]{4,2,1,0,3:T(8,128)}, u32[]{:S(2)}, u32[]{:S(2)}) %all-to-all-start) | async-done | bytes 6291488 | tf_op jit(solution)/shard_map/all_to_all | solution.py:83
  647.9 6.8 copy.19
  662.0 5.2 squeeze.5
  667.2 4.8 fusion.60
  690.3 4.7 subtract_bitcast_fusion
  695.0 14.4 %copy.10 = f32[3,8,16,128,16]{4,3,2,1,0:T(8,128)} copy(f32[3,8,16,128,16]{3,4,2,1,0:T(8,128)} %subtract_bitcast_fusion) | data formatting | bytes 6291456 | tf_op jit(solution)/shard_map/sub | solution.py:31
  709.4 21.8 %stack.47 = f32[1,3,8,16,2048]{4,3,2,1,0:T(8,128)} reshape(f32[3,8,16,128,16]{4,3,2,1,0:T(8,128)} %copy.10) | data formatting | bytes 6291456 | tf_op jit(solution)/shard_map/stack | solution.py:97
  731.2 12.5 %copy.11 = f32[3,8,16,128,16]{4,3,2,1,0:T(8,128)} copy(f32[3,8,16,128,16]{3,4,2,1,0:T(8,128)S(1)} %add_bitcast_fusion) | data formatting | bytes 6291456 | tf_op jit(solution)/shard_map/add | solution.py:34
  743.7 22.0 %stack.48 = f32[1,3,8,16,2048]{4,3,2,1,0:T(8,128)} reshape(f32[3,8,16,128,16]{4,3,2,1,0:T(8,128)} %copy.11) | data formatting | bytes 6291456 | tf_op jit(solution)/shard_map/stack | solution.py:97
  765.6 5.4 maximum_multiply_fusion
  (36 shorter events, 71.6 us)
Async XLA Ops:
  0.0 70.8 %collective-permute-start = (f32[3,8,64,512]{3,2,1,0:T(8,128)}, f32[3,8,64,512]{3,2,1,0:T(8,128)}, u32[]{:S(2)}, u32[]{:S(2)}) collective-permute-start(f32[3,8,64,512]{3,2,1,0:T(8,128)} %param.1), channel_id=1, source_target_pairs={{0,64},{4,68},{8,72},{12,76},{16,80},{20,84},{24,88},{28,92},{32,9... | collective-permute-start | bytes 9437192 | tf_op jit(solution)/shard_map/ppermute | solution.py:14
  78.1 135.8 %collective-permute-start.1 = (f32[2,3,8,64,512]{4,3,2,1,0:T(8,128)}, f32[2,3,8,64,512]{4,3,2,1,0:T(8,128)}, u32[]{:S(2)}, u32[]{:S(2)}) collective-permute-start(f32[2,3,8,64,512]{4,3,2,1,0:T(8,128)} %stack.40), channel_id=1, source_target_pairs={{0,32},{4,36},{8,40},{12,44},{16,48},{20,52},{24,56},{28,60},{32,0... | collective-permute-start | bytes 18874376 | tf_op jit(solution)/shard_map/ppermute | solution.py:14
  226.1 3.7 copy-start.2
  229.9 137.3 %collective-permute-start.2 = (f32[2,3,8,64,512]{4,3,2,1,0:T(8,128)}, f32[2,3,8,64,512]{4,3,2,1,0:T(8,128)}, u32[]{:S(2)}, u32[]{:S(2)}) collective-permute-start(f32[2,3,8,64,512]{4,3,2,1,0:T(8,128)} %pad_maximum_fusion), channel_id=1, source_target_pairs={{0,16},{4,20},{8,24},{12,28},{16,0},{20,4},{24,8},{28,12},{32,48},... | collective-permute-start | bytes 18874376 | tf_op jit(solution)/shard_map/ppermute | solution.py:14
  373.6 3.7 copy-start.3
  377.4 134.4 %collective-permute-start.3 = (f32[2,3,8,64,512]{4,3,2,1,0:T(8,128)}, f32[2,3,8,64,512]{4,3,2,1,0:T(8,128)}, u32[]{:S(2)}, u32[]{:S(2)}) collective-permute-start(f32[2,3,8,64,512]{4,3,2,1,0:T(8,128)} %pad_maximum_fusion.1), channel_id=1, source_target_pairs={{0,8},{4,12},{8,0},{12,4},{16,24},{20,28},{24,16},{28,20},{32,40},... | collective-permute-start | bytes 18874376 | tf_op jit(solution)/shard_map/ppermute | solution.py:14
  518.2 3.7 copy-start.1
  522.0 14.2 %collective-permute-start.4 = (f32[2,3,8,64,512]{4,3,2,1,0:T(8,128)}, f32[2,3,8,64,512]{4,3,2,1,0:T(8,128)}, u32[]{:S(2)}, u32[]{:S(2)}) collective-permute-start(f32[2,3,8,64,512]{4,3,2,1,0:T(8,128)} %pad_maximum_fusion.2), channel_id=1, source_target_pairs={{0,4},{4,0},{8,12},{12,8},{16,20},{20,16},{24,28},{28,24},{32,36},... | collective-permute-start | bytes 18874376 | tf_op jit(solution)/shard_map/ppermute | solution.py:14
  571.5 76.3 %all-to-all-start = ((f32[2,3,8,64,512]{4,2,1,0,3:T(8,128)}), f32[2,3,8,64,512]{4,2,1,0,3:T(8,128)}, u32[]{:S(2)}, u32[]{:S(2)}) async-start(f32[2,3,8,64,512]{4,2,1,0,3:T(8,128)} %copy.8), calls=%async_computation | async-start | bytes 12582912 | tf_op jit(solution)/shard_map/all_to_all | solution.py:83
  675.0 3.0 copy-start
  743.7 22.0 %copy-start.4 = (f32[1,3,8,16,2048]{4,3,2,1,0:T(8,128)S(1)}, f32[1,3,8,16,2048]{4,3,2,1,0:T(8,128)}, u32[]{:S(2)}) copy-start(f32[1,3,8,16,2048]{4,3,2,1,0:T(8,128)} %stack.47) | copy-start | bytes 9437188
where the time goes:
time: 781 us; the launch traced here: 772 us
  waiting for transfers between devices  552 us (71%)
  local copies, waits for them, and re-layouts  99.8 us (13%)
  other arithmetic  57.6 us (7%)
  matrix products  44.8 us (6%)
  starting transfers between devices  15.6 us (2%)
    ppermute x5, waiting for transfers between devices, swapped(): return lax.ppermute(value, axis, pairs)  481 us
    all_to_all x1, waiting for transfers between devices, per_device(): lax.all_to_all(spectrum_x, 'gy', split_axis=3, concat_axis=4, tiled=True)  71 us
    another operation x2, local copies, waits for them, and re-layouts, per_device(): result = jnp.stack([last_re, last_im]) * scale  43.7 us
    select_n x4, other arithmetic, per_device(): upper_part = jnp.where(upper, partial_value, other)  23.4 us
  transfers between devices with their start and end apart: 6, of which 6 were waited for; matrix products, arithmetic and copies ran while one was open for 0% of the time, Pallas kernels for 0%

commit v1 on v0

v1 whole, which is shorter than its diff:
```python
import functools
import math

import jax
import jax.numpy as jnp
import ml_dtypes
import numpy as np
from jax import lax
from jax.experimental import pallas as pl
from jax.experimental.pallas import tpu as pltpu
from jax.sharding import PartitionSpec as P

MESH = pl.DeviceIdType.MESH
F32 = jnp.float32
BF16 = jnp.bfloat16
LANES = 128
SUB = 8
CHUNKS = 8
LAG_B = 2
LAG_C = 4


def bit_reverse(value, digits):
    return int(format(value, "0%db" % digits)[::-1], 2)


def cadd(a, b):
    im = a[1] if b[1] is None else b[1] if a[1] is None else a[1] + b[1]
    return (a[0] + b[0], im)


def csub(a, b):
    im = a[1] if b[1] is None else -b[1] if a[1] is None else a[1] - b[1]
    return (a[0] - b[0], im)


def conj(a):
    return (a[0], None if a[1] is None else -a[1])


def turn(a, k, n):
    k = k % n
    re, im = a
    if k == 0:
        return a
    if 4 * k == n:
        return (jnp.zeros_like(re) if im is None else im, -re)
    if 8 * k == n:
        h = math.sqrt(0.5)
        if im is None:
            return (re * h, re * -h)
        return ((re + im) * h, (im - re) * h)
    if 8 * k == 3 * n:
        h = math.sqrt(0.5)
        if im is None:
            return (re * -h, re * -h)
        return ((im - re) * h, (re + im) * -h)
    c, s = math.cos(2 * math.pi * k / n), -math.sin(2 * math.pi * k / n)
    if im is None:
        return (re * c, re * s)
    return (re * c - im * s, re * s + im * c)


def real_fft(values):
    n = len(values)
    if n == 1:
        return [(values[0], None)]
    if n == 2:
        return [(values[0] + values[1], None), (values[0] - values[1], None)]
    even, odd = real_fft(values[0::2]), real_fft(values[1::2])
    out = [None] * (n // 2 + 1)
    for k in range(n // 4 + 1):
        t = turn(odd[k], k, n)
        if 4 * k == n:
            out[k] = (even[k][0], -odd[k][0])
            continue
        out[k] = cadd(even[k], t)
        out[n // 2 - k] = conj(csub(even[k], t))
    return out


def complex_fft(values):
    n = len(values)
    if n == 1:
        return values
    even, odd = complex_fft(values[0::2]), complex_fft(values[1::2])
    out = [None] * n
    for k in range(n // 2):
        t = turn(odd[k], k, n)
        out[k] = cadd(even[k], t)
        out[k + n // 2] = csub(even[k], t)
    return out


def split(value):
    high = value.astype(BF16)
    return high, (value - high.astype(F32)).astype(BF16)


def split_table(table):
    high = table.astype(np.float32).astype(ml_dtypes.bfloat16)
    low = (table - high.astype(np.float64)).astype(ml_dtypes.bfloat16)
    return high, low


def root(phase, n):
    angle = -2.0 * np.pi * (phase % n) / n
    return np.cos(angle), np.sin(angle)


def tables(gx, gy, rows, cols, freqs):
    nx, ny = gx * rows, gy * cols
    groups = ny // LANES
    share = cols // groups
    per = LANES // share
    cell = np.arange(cols)
    a, e = cell // groups, cell % groups
    perm = np.zeros((gy, cols, cols), np.float32)
    for s in range(gy):
        place = e // per * LANES + (e % per + s) % per * share + a
        perm[s, cell, place] = 1.0
    tiles = rows // SUB
    m = np.arange(rows).reshape(tiles, 1, SUB)
    r = np.array([bit_reverse(i, gx.bit_length() - 1) for i in range(gx)]).reshape(1, gx, 1)
    turn_x = np.stack(root(m * r, nx), axis=2)
    turn_x = np.broadcast_to(turn_x[..., None], turn_x.shape + (LANES,))
    c, s = root(np.outer(np.arange(rows), np.arange(rows)), rows)
    dft_x = np.block([[c, -s], [s, c]])
    xh, xl = split_table(dft_x)
    x_first = np.concatenate([xh, xh], axis=1)
    dft_y = []
    lane = np.arange(LANES)
    for q in range(per):
        spot = (lane // share - q) % per * share + lane % share
        c, s = root(np.outer(spot, lane), LANES)
        dft_y.append(np.block([[c, s], [-s, c]]))
    dft_y = np.stack(dft_y) / math.sqrt(nx * ny)
    yh, yl = split_table(dft_y)
    turn_y = np.stack(root(np.outer(np.arange(groups), lane), ny), axis=1)
    turn_y = np.broadcast_to(turn_y[:, :, None, :], (groups, 2, SUB, LANES))
    return (
        perm.astype(ml_dtypes.bfloat16),
        np.ascontiguousarray(turn_x, np.float32),
        x_first,
        xl,
        yh,
        yl,
        np.ascontiguousarray(turn_y, np.float32),
    )


def kernel(
    gx, gy, planes, chunks,
    field, perm_hbm, turnx_hbm, xfirst_hbm, xlow_hbm, yhigh_hbm, ylow_hbm, turny_hbm,
    out,
    raw, s1, r1, s2, r2, s3, r3, zed, stage, perm, turnx, xfirst, xlow, yhigh, ylow, turny,
    in_sem, tab_sem, ss1, rs1, ss2, rs2, ss3, rs3, out_sem,
):
    me, my = lax.axis_index("gx"), lax.axis_index("gy")
    step = planes // chunks
    rows, cols = raw.shape[1:]
    tiles, wide = rows // SUB, cols // LANES
    freqs = r3.shape[3]
    groups = turny.shape[0]
    per = yhigh.shape[0]

    def part(c):
        return pl.ds(c * step, step)

    def load(c):
        return pltpu.make_async_copy(field.at[part(c)], raw.at[part(c)], in_sem.at[c])

    loads = [
        pltpu.make_async_copy(a, b, tab_sem.at[i])
        for i, (a, b) in enumerate(
            [
                (perm_hbm.at[my], perm),
                (turnx_hbm.at[me // wide], turnx),
                (xfirst_hbm, xfirst),
                (xlow_hbm, xlow),
                (yhigh_hbm, yhigh),
                (ylow_hbm, ylow),
                (turny_hbm, turny),
            ]
        )
    ]

    barrier = pltpu.get_barrier_semaphore()

    def greet(i, _):
        pl.semaphore_signal(barrier, inc=1, device_id=(lax.rem(me + i, gx), my), device_id_type=MESH)
        return 0

    lax.fori_loop(1, gx, greet, 0)
    for j in range(1, gy):
        pl.semaphore_signal(barrier, inc=1, device_id=(me, lax.rem(my + j, gy)), device_id_type=MESH)
    loads[0].start()
    lax.fori_loop(0, chunks, lambda c, _: (load(c).start(), 0)[1], 0)
    for copy in loads[1:]:
        copy.start()
    pl.semaphore_wait(barrier, gx + gy - 2)
    loads[0].wait()

    def exchange_x(c, source, target, send, recv):
        pltpu.make_async_copy(source.at[me, part(c)], target.at[me, part(c)], recv.at[c]).start()

        def one(i, _):
            t = lax.rem(me + i, gx)
            pltpu.make_async_remote_copy(
                src_ref=source.at[t, part(c)],
                dst_ref=target.at[me, part(c)],
                send_sem=send.at[c],
                recv_sem=recv.at[c],
                device_id=(t, my),
                device_id_type=MESH,
            ).start()
            return 0

        lax.fori_loop(1, gx, one, 0)

    def exchange_y(c):
        pltpu.make_async_copy(s3.at[my, part(c)], r3.at[my, part(c)], rs3.at[c]).start()
        for j in range(1, gy):
            t = lax.rem(my + j, gy)
            pltpu.make_async_remote_copy(
                src_ref=s3.at[t, part(c)],
                dst_ref=r3.at[my, part(c)],
                send_sem=ss3.at[c],
                recv_sem=rs3.at[c],
                device_id=(me, t),
                device_id_type=MESH,
            ).start()

    def arrived(c, target, recv):
        pltpu.make_async_copy(target.at[:, part(c)], target.at[:, part(c)], recv.at[c]).wait()

    def sent(c, source, send):
        some = source.at[pl.ds(1, source.shape[0] - 1), part(c)]
        pltpu.make_async_copy(some, some, send.at[c]).wait()

    def permute(c):
        load(c).wait()

        def one(p, _):
            plane = c * step + p
            high, low = split(raw[plane])
            both = jnp.dot(jnp.concatenate([high, low], axis=0), perm[...], preferred_element_type=F32)
            moved = both[:rows] + both[rows:]
            for t in range(tiles):
                for w in range(wide):
                    s1[t * wide + w, plane] = moved[t * SUB : (t + 1) * SUB, w * LANES : (w + 1) * LANES]
            return 0

        lax.fori_loop(0, step, one, 0)

    def over_gx(c):
        def one(p, _):
            plane = c * step + p
            got = real_fft([r1[g, plane] for g in range(gx)])
            for i in range(gx):
                r = bit_reverse(i, gx.bit_length() - 1)
                re, im = got[r] if 2 * r <= gx else conj(got[gx - r])
                if r == 0:
                    s2[i, plane, 0] = re
                    s2[i, plane, 1] = jnp.zeros_like(re)
                    continue
                tr, ti = turnx[i, 0], turnx[i, 1]
                if im is None:
                    s2[i, plane, 0] = re * tr
                    s2[i, plane, 1] = re * ti
                else:
                    s2[i, plane, 0] = re * tr - im * ti
                    s2[i, plane, 1] = re * ti + im * tr
            return 0

        lax.fori_loop(0, step, one, 0)

    def over_m(c):
        def one(p, _):
            plane = c * step + p
            value = jnp.concatenate(
                [
                    jnp.concatenate(
                        [r2[t * wide + w, plane, part_] for part_ in range(2) for t in range(tiles)], axis=0
                    )
                    for w in range(wide)
                ],
                axis=1,
            )
            high, low = split(value)
            done = jnp.dot(xfirst[...], jnp.concatenate([high, low], axis=0), preferred_element_type=F32)
            done = done + jnp.dot(xlow[...], high, preferred_element_type=F32)
            for part_ in range(2):
                for s in range(gy):
                    first = part_ * rows + s * freqs
                    s3[s, plane, part_] = done[first : first + freqs]
            return 0

        lax.fori_loop(0, step, one, 0)

    def result(c):
        slot = lax.rem(c, 2)
        return pltpu.make_async_copy(stage.at[slot], out.at[:, part(c)], out_sem.at[slot])

    def over_y(c):
        slot = lax.rem(c, 2)
        group = lax.broadcasted_iota(jnp.int32, (freqs, LANES), 1) // (LANES // per)

        def one(p, _):
            plane = c * step + p
            for q in range(per):
                lines = []
                for w in range(wide):
                    halves = []
                    for part_ in range(2):
                        got = [r3[s, plane, part_, :, w * LANES : (w + 1) * LANES] for s in range(gy)]
                        merged = got[-q % per]
                        for g in range(1, per):
                            merged = jnp.where(group == g, got[(g - q) % per], merged)
                        halves.append(merged)
                    lines.append(jnp.concatenate(halves, axis=1))
                high, low = split(jnp.concatenate(lines, axis=0))
                both = jnp.dot(jnp.concatenate([high, low], axis=0), yhigh[q], preferred_element_type=F32)
                total = wide * freqs
                done = both[:total] + both[total:] + jnp.dot(high, ylow[q], preferred_element_type=F32)
                for w in range(wide):
                    zed[w * per + q] = done[w * freqs : (w + 1) * freqs]
            for b in range(freqs // SUB):
                at = slice(b * SUB, (b + 1) * SUB)
                values = []
                for e in range(groups):
                    re, im = zed[e, at, :LANES], zed[e, at, LANES:]
                    if e == 0:
                        values.append((re, im))
                    else:
                        tr, ti = turny[e, 0], turny[e, 1]
                        values.append((re * tr - im * ti, re * ti + im * tr))
                for k, (re, im) in enumerate(complex_fft(values)):
                    stage[slot, 0, p, at, k * LANES : (k + 1) * LANES] = re
                    stage[slot, 1, p, at, k * LANES : (k + 1) * LANES] = im
            return 0

        lax.fori_loop(0, step, one, 0)

    def enter(c, _):
        permute(c)
        exchange_x(c, s1, r1, ss1, rs1)
        return 0

    lax.fori_loop(0, chunks, enter, 0)
    for copy in loads[1:]:
        copy.wait()

    def turn_step(i, _):
        @pl.when(i < chunks)
        def _():
            arrived(i, r1, rs1)
            over_gx(i)
            exchange_x(i, s2, r2, ss2, rs2)

        @pl.when(jnp.logical_and(i >= LAG_B, i < chunks + LAG_B))
        def _():
            c = i - LAG_B
            arrived(c, r2, rs2)
            over_m(c)
            exchange_y(c)

        @pl.when(i >= LAG_C)
        def _():
            c = i - LAG_C
            arrived(c, r3, rs3)

            @pl.when(c >= 2)
            def _():
                result(c - 2).wait()

            over_y(c)
            result(c).start()

        return 0

    lax.fori_loop(0, chunks + LAG_C, turn_step, 0)

    def finish(c, _):
        sent(c, s1, ss1)
        sent(c, s2, ss2)
        sent(c, s3, ss3)
        return 0

    lax.fori_loop(0, chunks, finish, 0)
    for c in (chunks - 2, chunks - 1):
        result(c).wait()


def solution(mesh):
    gx, gy = mesh.shape["gx"], mesh.shape["gy"]

    def per_device(field):
        comp, depth, rows, cols = field.shape
        planes = comp * depth
        freqs = rows // gy
        ny = gy * cols
        groups = ny // LANES
        step = planes // CHUNKS
        consts = tables(gx, gy, rows, cols, freqs)
        any_ = pl.BlockSpec(memory_space=pl.ANY)
        pieces = (rows // SUB) * (cols // LANES)
        assert pieces == gx
        vmem = lambda a: pltpu.VMEM(a.shape, a.dtype)
        dma = pltpu.SemaphoreType.DMA
        perm, turnx, xfirst, xlow, yhigh, ylow, turny = consts
        result = pl.pallas_call(
            functools.partial(kernel, gx, gy, planes, CHUNKS),
            out_shape=jax.ShapeDtypeStruct((2, planes, freqs, ny), F32),
            in_specs=[any_] * 8,
            out_specs=any_,
            scratch_shapes=[
                pltpu.VMEM((planes, rows, cols), F32),
                pltpu.VMEM((gx, planes, SUB, LANES), F32),
                pltpu.VMEM((gx, planes, SUB, LANES), F32),
                pltpu.VMEM((gx, planes, 2, SUB, LANES), F32),
                pltpu.VMEM((gx, planes, 2, SUB, LANES), F32),
                pltpu.VMEM((gy, planes, 2, freqs, cols), F32),
                pltpu.VMEM((gy, planes, 2, freqs, cols), F32),
                pltpu.VMEM((groups, freqs, 2 * LANES), F32),
                pltpu.VMEM((2, 2, step, freqs, ny), F32),
                pltpu.VMEM(perm.shape[1:], perm.dtype),
                pltpu.VMEM(turnx.shape[1:], turnx.dtype),
                vmem(xfirst),
                vmem(xlow),
                vmem(yhigh),
                vmem(ylow),
                vmem(turny),
                dma((CHUNKS,)),
                dma((7,)),
                dma((CHUNKS,)),
                dma((CHUNKS,)),
                dma((CHUNKS,)),
                dma((CHUNKS,)),
                dma((CHUNKS,)),
                dma((CHUNKS,)),
                dma((2,)),
            ],
            compiler_params=pltpu.CompilerParams(
                collective_id=0, has_side_effects=True, vmem_limit_bytes=56 << 20
            ),
        )(field.reshape(planes, rows, cols), *[jnp.asarray(c) for c in consts])
        return result.reshape(2, comp, depth, freqs, ny)

    return jax.shard_map(
        per_device,
        mesh=mesh,
        in_specs=(P(None, None, "gx", "gy"),),
        out_specs=P(None, None, None, ("gx", "gy"), None),
        check_vma=False,
    )
```

time: 781 us -> 166 us (0.21); the launches traced: 772 us -> 166 us
  waiting for transfers between devices: 552 us -> 0 us
  Pallas kernels: 0 us -> 160 us
  local copies, waits for them, and re-layouts: 99.8 us -> 6.29 us
  other arithmetic: 57.6 us -> 0 us
  matrix products: 44.8 us -> 0 us
  starting transfers between devices: 15.6 us -> 0 us
    ppermute x5 -> x0, waiting for transfers between devices: 481 us -> none  [swapped(): return lax.ppermute(value, axis, pairs)]
    pallas_call x0 -> x1, Pallas kernels: none -> 160 us  [per_device(): pl.pallas_call(functools.partial(kernel, gx, gy, planes, CHUNKS), out_sha...]
    all_to_all x1 -> x0, waiting for transfers between devices: 71 us -> none  [per_device(): lax.all_to_all(spectrum_x, 'gy', split_axis=3, concat_axis=4, tiled=True)]
    another operation x4 -> x0, local copies, waits for them, and re-layouts: 53.6 us -> none  [the longest x2 43.7 us: per_device(): result = jnp.stack([last_re, last_im]) * scale]
    dot_general x12 -> x0, matrix products: 44.8 us -> none  [the longest x3 12.9 us: complex_apply(): jnp.einsum(form, table_re, data_im, precision=HIGH)]
    select_n x4 -> x0, other arithmetic: 23.4 us -> none  [per_device(): upper_part = jnp.where(upper, partial_value, other)]
    another operation x5 -> x0, other arithmetic: 16.1 us -> none  [the longest x3 11.2 us: per_device(): jnp.stack([lower_part[0] + twist_re * upper_part[0] - twist_im * upper_pa...]
    sub x1 -> x0, local copies, waits for them, and re-layouts: 14.4 us -> none  [complex_apply(): jnp.einsum(form, table_re, data_re, precision=HIGH)]
  transfers between devices with their start and end apart: 6 -> 0, of which waited for: 6 -> 0; matrix products, arithmetic and copies ran while one was open for 0% -> 0% of each run, Pallas kernels for 0% -> 0%
where the time goes in v1:
time: 166 us
  Pallas kernels  160 us (96%)
  local copies, waits for them, and re-layouts  6.29 us (4%)
    pallas_call x1, Pallas kernels, per_device(): pl.pallas_call(functools.partial(kernel, gx, gy, planes, CHUNKS), out_sha...  160 us
    unnamed x1, local copies, waits for them, and re-layouts  6.29 us

profile of v1, /device:TPU:3, one launch (start us, length us, event | category | flops | bytes accessed | tf_op | source)
XLA Modules:
  0.0 166.0 jit_solution(2643118767978637430)
XLA Ops:
  0.0 159.7 %shard_map.82 = f32[2,24,16,2048]{3,2,1,0:T(8,128)} custom-call(f32[24,64,512]{2,1,0:T(8,128)} %bitcast.3, bf16[4,512,512]{2,1,0:T(8,128)(2,1)} %constant.14.clone.perm_hbm, f32[8,32,2,8,128]{4,3,2,1,0:T(8,128)} %constant.15.clone.turnx_hbm, bf16[128,256]{1,0:T(8,128)(2,1)} %constant.16.clone.xfirst_hbm, bf16[128,128]{1,0:T(8,128)(2,1)} %constant.17.clone.xlow_hbm, ...), custom_call_target="tpu_custom_call" | custom-call | tf_op jit(solution)/shard_map/pallas_call | solution.py:412
  159.7 6.3 %copy.10 = f32[2,3,8,16,2048]{4,3,2,1,0:T(8,128)} copy(f32[2,3,8,16,2048]{4,3,2,1,0:T(8,128)} %bitcast.2) | data formatting | bytes 12582912

commit v2 on v1

--- a/solution.py
+++ b/solution.py
@@ -15,7 +15,7 @@
 BF16 = jnp.bfloat16
 LANES = 128
 SUB = 8
-CHUNKS = 8
+CHUNKS = 24
 LAG_B = 2
 LAG_C = 4
 

time: 166 us -> 129 us (0.78); the launches traced: 166 us -> 127 us
  Pallas kernels: 160 us -> 121 us
    pallas_call x1, Pallas kernels: 160 us -> 121 us  [per_device(): pl.pallas_call(functools.partial(kernel, gx, gy, planes, CHUNKS), out_sha...]
where the time goes in v2:
time: 129 us; the launch traced here: 127 us
  Pallas kernels  121 us (94%)
  local copies, waits for them, and re-layouts  6.29 us (5%)
    pallas_call x1, Pallas kernels, per_device(): pl.pallas_call(functools.partial(kernel, gx, gy, planes, CHUNKS), out_sha...  121 us
    unnamed x1, local copies, waits for them, and re-layouts  6.29 us

profile of v2, /device:TPU:3, one launch (start us, length us, event | category | flops | bytes accessed | tf_op | source)
XLA Modules:
  0.0 126.9 jit_solution(11517667807003968114)
XLA Ops:
  0.0 120.6 %shard_map.82 = f32[2,24,16,2048]{3,2,1,0:T(8,128)} custom-call(f32[24,64,512]{2,1,0:T(8,128)} %bitcast.3, bf16[4,512,512]{2,1,0:T(8,128)(2,1)} %constant.14.clone.perm_hbm, f32[8,32,2,8,128]{4,3,2,1,0:T(8,128)} %constant.15.clone.turnx_hbm, bf16[128,256]{1,0:T(8,128)(2,1)} %constant.16.clone.xfirst_hbm, bf16[128,128]{1,0:T(8,128)(2,1)} %constant.17.clone.xlow_hbm, ...), custom_call_target="tpu_custom_call" | custom-call | tf_op jit(solution)/shard_map/pallas_call | solution.py:412
  120.6 6.3 %copy.10 = f32[2,3,8,16,2048]{4,3,2,1,0:T(8,128)} copy(f32[2,3,8,16,2048]{4,3,2,1,0:T(8,128)} %bitcast.2) | data formatting | bytes 12582912

commit v3 on v2

v3 whole, which is shorter than its diff:
```python
import functools
import math

import jax
import jax.numpy as jnp
import ml_dtypes
import numpy as np
from jax import lax
from jax.experimental import pallas as pl
from jax.experimental.pallas import tpu as pltpu
from jax.sharding import PartitionSpec as P

MESH = pl.DeviceIdType.MESH
F32 = jnp.float32
BF16 = jnp.bfloat16
LANES = 128
SUB = 8
WRITES = 8
PLACES = (2, 8, 4, 16)
FAMILIES = len(PLACES)
AHEAD = 6
LAG_A = 4
LAG_B = 7
LAG_C = 9


def bit_reverse(value, digits):
    return int(format(value, "0%db" % digits)[::-1], 2)


def cadd(a, b):
    im = a[1] if b[1] is None else b[1] if a[1] is None else a[1] + b[1]
    return (a[0] + b[0], im)


def csub(a, b):
    im = a[1] if b[1] is None else -b[1] if a[1] is None else a[1] - b[1]
    return (a[0] - b[0], im)


def conj(a):
    return (a[0], None if a[1] is None else -a[1])


def turn(a, k, n):
    k = k % n
    re, im = a
    if k == 0:
        return a
    if 4 * k == n:
        return (jnp.zeros_like(re) if im is None else im, -re)
    if 8 * k == n:
        h = math.sqrt(0.5)
        if im is None:
            return (re * h, re * -h)
        return ((re + im) * h, (im - re) * h)
    if 8 * k == 3 * n:
        h = math.sqrt(0.5)
        if im is None:
            return (re * -h, re * -h)
        return ((im - re) * h, (re + im) * -h)
    c, s = math.cos(2 * math.pi * k / n), -math.sin(2 * math.pi * k / n)
    if im is None:
        return (re * c, re * s)
    return (re * c - im * s, re * s + im * c)


def real_fft(values):
    n = len(values)
    if n == 1:
        return [(values[0], None)]
    if n == 2:
        return [(values[0] + values[1], None), (values[0] - values[1], None)]
    even, odd = real_fft(values[0::2]), real_fft(values[1::2])
    out = [None] * (n // 2 + 1)
    for k in range(n // 4 + 1):
        t = turn(odd[k], k, n)
        if 4 * k == n:
            out[k] = (even[k][0], -odd[k][0])
            continue
        out[k] = cadd(even[k], t)
        out[n // 2 - k] = conj(csub(even[k], t))
    return out


def complex_fft(values):
    n = len(values)
    if n == 1:
        return values
    even, odd = complex_fft(values[0::2]), complex_fft(values[1::2])
    out = [None] * n
    for k in range(n // 2):
        t = turn(odd[k], k, n)
        out[k] = cadd(even[k], t)
        out[k + n // 2] = csub(even[k], t)
    return out


def split(value):
    high = value.astype(BF16)
    return high, (value - high.astype(F32)).astype(BF16)


def split_table(table):
    high = table.astype(np.float32).astype(ml_dtypes.bfloat16)
    low = (table - high.astype(np.float64)).astype(ml_dtypes.bfloat16)
    return high, low


def root(phase, n):
    angle = -2.0 * np.pi * (phase % n) / n
    return np.cos(angle), np.sin(angle)


def tables(gx, gy, rows, cols, freqs):
    nx, ny = gx * rows, gy * cols
    groups = ny // LANES
    share = cols // groups
    per = LANES // share
    cell = np.arange(cols)
    a, e = cell // groups, cell % groups
    perm = np.zeros((gy, cols, cols), np.float32)
    for s in range(gy):
        place = e // per * LANES + (e % per + s) % per * share + a
        perm[s, cell, place] = 1.0
    tiles = rows // SUB
    m = np.arange(rows).reshape(tiles, 1, SUB)
    r = np.array([bit_reverse(i, gx.bit_length() - 1) for i in range(gx)]).reshape(1, gx, 1)
    turn_x = np.stack(root(m * r, nx), axis=2)
    turn_x = np.broadcast_to(turn_x[..., None], turn_x.shape + (LANES,))
    c, s = root(np.outer(np.arange(rows), np.arange(rows)), rows)
    dft_x = np.block([[c, -s], [s, c]])
    xh, xl = split_table(dft_x)
    x_first = np.concatenate([xh, xh], axis=1)
    dft_y = []
    lane = np.arange(LANES)
    for q in range(per):
        spot = (lane // share - q) % per * share + lane % share
        c, s = root(np.outer(spot, lane), LANES)
        dft_y.append(np.block([[c, s], [-s, c]]))
    dft_y = np.stack(dft_y) / math.sqrt(nx * ny)
    yh, yl = split_table(dft_y)
    turn_y = np.stack(root(np.outer(np.arange(groups), lane), ny), axis=1)
    turn_y = np.broadcast_to(turn_y[:, :, None, :], (groups, 2, SUB, LANES))
    return (
        perm.astype(ml_dtypes.bfloat16),
        np.ascontiguousarray(turn_x, np.float32),
        x_first,
        xl,
        yh,
        yl,
        np.ascontiguousarray(turn_y, np.float32),
    )


def gray(g):
    x1, x0, z1, z0, c = g // 16, g // 8 % 2, g // 4 % 2, g // 2 % 2, g % 2
    return x1 * 16 + (x1 + x0) % 2 * 8 + z1 * 4 + (z1 + z0) % 2 * 2 + c


def ungray(code):
    x1, xv, z1, zv, c = code // 16, code // 8 % 2, code // 4 % 2, code // 2 % 2, code % 2
    return x1 * 16 + (x1 + xv) % 2 * 8 + z1 * 4 + (z1 + zv) % 2 * 2 + c


def kernel(
    gx, gy, planes,
    field, perm_hbm, turnx_hbm, xfirst_hbm, xlow_hbm, yhigh_hbm, ylow_hbm, turny_hbm,
    out,
    raw, s1, r1, s2, r2, s3, r3, zed, perm, turnx, xfirst, xlow, yhigh, ylow, turny,
    in_sem, tab_sem, ss1, rs1, ssf, rsf, ss2, rs2, ss3, rs3,
):
    me, my = lax.axis_index("gx"), lax.axis_index("gy")
    code = gray(me)
    rows, cols = raw.shape[1:]
    tiles, wide = rows // SUB, cols // LANES
    freqs = r3.shape[3]
    groups = turny.shape[0]
    per = yhigh.shape[0]
    half = gx // 2

    def bit_of(family):
        place = PLACES[0]
        for f in range(1, FAMILIES):
            place = jnp.where(family == f, PLACES[f], place)
        return place, code // place % 2

    def piece(place):
        return code // (2 * place) * place + code % place

    def device(index, place, bit):
        return ungray(index // place * (2 * place) + bit * place + index % place)

    def load(c):
        return pltpu.make_async_copy(field.at[c], raw.at[c], in_sem.at[c])

    pairs = [(perm_hbm.at[my], perm)]
    for f in range(FAMILIES):
        pairs.append((turnx_hbm.at[piece(PLACES[f]) * 2 // wide], turnx.at[f]))
    pairs += [
        (xfirst_hbm, xfirst),
        (xlow_hbm, xlow),
        (yhigh_hbm, yhigh),
        (ylow_hbm, ylow),
        (turny_hbm, turny),
    ]
    loads = [pltpu.make_async_copy(a, b, tab_sem.at[i]) for i, (a, b) in enumerate(pairs)]

    barrier = pltpu.get_barrier_semaphore()

    def greet(i, _):
        pl.semaphore_signal(barrier, inc=1, device_id=(lax.rem(me + i, gx), my), device_id_type=MESH)
        return 0

    lax.fori_loop(1, gx, greet, 0)
    for j in range(1, gy):
        pl.semaphore_signal(barrier, inc=1, device_id=(me, lax.rem(my + j, gy)), device_id_type=MESH)
    loads[0].start()
    lax.fori_loop(0, planes, lambda c, _: (load(c).start(), 0)[1], 0)
    for copy in loads[1:]:
        copy.start()
    pl.semaphore_wait(barrier, gx + gy - 2)
    loads[0].wait()

    def send(source, target, send_sem, recv_sem, device_id):
        pltpu.make_async_remote_copy(
            src_ref=source,
            dst_ref=target,
            send_sem=send_sem,
            recv_sem=recv_sem,
            device_id=device_id,
            device_id_type=MESH,
        ).start()

    def wait(ref, sem):
        pltpu.make_async_copy(ref, ref, sem).wait()

    def exchange_raw(c):
        place, bit = bit_of(lax.rem(c, FAMILIES))
        own = piece(place)
        pltpu.make_async_copy(s1.at[c, pl.ds(2 * own, 2)], r1.at[c, me], rs1.at[c]).start()

        def one(k, _):
            i = lax.rem(own + k, half)
            send(s1.at[c, pl.ds(2 * i, 2)], r1.at[c, me], ss1.at[c], rs1.at[c], (device(i, place, bit), my))
            return 0

        lax.fori_loop(1, half, one, 0)

    def forward(c):
        place, bit = bit_of(lax.rem(c, FAMILIES))
        other = ungray(code + place - 2 * place * bit)

        def one(i, _):
            g = device(i, place, bit)
            send(r1.at[c, g], r1.at[c, g], ssf.at[c], rsf.at[c], (other, my))
            return 0

        lax.fori_loop(0, half, one, 0)

    def exchange_x(c):
        place, bit = bit_of(lax.rem(c, FAMILIES))
        own = piece(place)
        pltpu.make_async_copy(s2.at[c, me], r2.at[c, own], rs2.at[c]).start()

        def one(k, _):
            t = device(lax.rem(own + k, half), place, bit)
            send(s2.at[c, t], r2.at[c, own], ss2.at[c], rs2.at[c], (t, my))
            return 0

        lax.fori_loop(1, half, one, 0)

    def exchange_y(c):
        pltpu.make_async_copy(s3.at[my, c], r3.at[my, c], rs3.at[c]).start()
        for j in range(1, gy):
            t = lax.rem(my + j, gy)
            send(s3.at[t, c], r3.at[my, c], ss3.at[c], rs3.at[c], (me, t))

    def permute(c):
        load(c).wait()
        high, low = split(raw[c])
        both = jnp.dot(jnp.concatenate([high, low], axis=0), perm[...], preferred_element_type=F32)
        moved = both[:rows] + both[rows:]
        for t in range(tiles):
            for w in range(wide):
                s1[c, t * wide + w] = moved[t * SUB : (t + 1) * SUB, w * LANES : (w + 1) * LANES]

    def over_gx(c):
        family = lax.rem(c, FAMILIES)

        def one(w, _):
            got = real_fft([r1[c, g, w] for g in range(gx)])
            for i in range(gx):
                r = bit_reverse(i, gx.bit_length() - 1)
                re, im = got[r] if 2 * r <= gx else conj(got[gx - r])
                if r == 0:
                    s2[c, i, w, 0] = re
                    s2[c, i, w, 1] = jnp.zeros_like(re)
                    continue
                tr, ti = turnx[family, i, 0], turnx[family, i, 1]
                if im is None:
                    s2[c, i, w, 0] = re * tr
                    s2[c, i, w, 1] = re * ti
                else:
                    s2[c, i, w, 0] = re * tr - im * ti
                    s2[c, i, w, 1] = re * ti + im * tr
            return 0

        lax.fori_loop(0, 2, one, 0)

    def over_m(c):
        value = jnp.concatenate(
            [
                jnp.concatenate(
                    [r2[c, (t * wide + w) // 2, w % 2, part] for part in range(2) for t in range(tiles)], axis=0
                )
                for w in range(wide)
            ],
            axis=1,
        )
        high, low = split(value)
        done = jnp.dot(xfirst[...], jnp.concatenate([high, low], axis=0), preferred_element_type=F32)
        done = done + jnp.dot(xlow[...], high, preferred_element_type=F32)
        for part in range(2):
            for s in range(gy):
                first = part * rows + s * freqs
                s3[s, c, part] = done[first : first + freqs]

    def over_y(c):
        group = lax.broadcasted_iota(jnp.int32, (freqs, LANES), 1) // (LANES // per)
        for q in range(per):
            lines = []
            for w in range(wide):
                halves = []
                for part in range(2):
                    got = [r3[s, c, part, :, w * LANES : (w + 1) * LANES] for s in range(gy)]
                    merged = got[-q % per]
                    for g in range(1, per):
                        merged = jnp.where(group == g, got[(g - q) % per], merged)
                    halves.append(merged)
                lines.append(jnp.concatenate(halves, axis=1))
            high, low = split(jnp.concatenate(lines, axis=0))
            both = jnp.dot(jnp.concatenate([high, low], axis=0), yhigh[q], preferred_element_type=F32)
            total = wide * freqs
            done = both[:total] + both[total:] + jnp.dot(high, ylow[q], preferred_element_type=F32)
            for w in range(wide):
                zed[w * per + q] = done[w * freqs : (w + 1) * freqs]
        for b in range(freqs // SUB):
            at = slice(b * SUB, (b + 1) * SUB)
            values = []
            for e in range(groups):
                re, im = zed[e, at, :LANES], zed[e, at, LANES:]
                if e == 0:
                    values.append((re, im))
                else:
                    tr, ti = turny[e, 0], turny[e, 1]
                    values.append((re * tr - im * ti, re * ti + im * tr))
            for k, (re, im) in enumerate(complex_fft(values)):
                out[0, c, at, k * LANES : (k + 1) * LANES] = re
                out[1, c, at, k * LANES : (k + 1) * LANES] = im

    def enter(c, _):
        permute(c)
        exchange_raw(c)
        return 0

    lax.fori_loop(0, AHEAD, enter, 0)
    for copy in loads[1:]:
        copy.wait()

    def turn_step(i, _):
        @pl.when(i < planes - AHEAD)
        def _():
            enter(i + AHEAD, 0)

        @pl.when(i < planes)
        def _():
            wait(r1.at[i, pl.ds(0, half)], rs1.at[i])
            forward(i)

        @pl.when(jnp.logical_and(i >= LAG_A, i < planes + LAG_A))
        def _():
            c = i - LAG_A
            wait(r1.at[c, pl.ds(0, half)], rsf.at[c])
            over_gx(c)
            exchange_x(c)

        @pl.when(jnp.logical_and(i >= LAG_B, i < planes + LAG_B))
        def _():
            c = i - LAG_B
            wait(r2.at[c], rs2.at[c])
            over_m(c)
            exchange_y(c)

        @pl.when(i >= LAG_C)
        def _():
            c = i - LAG_C
            wait(r3.at[:, c], rs3.at[c])
            over_y(c)

        return 0

    lax.fori_loop(0, planes + LAG_C, turn_step, 0)

    def finish(c, _):
        wait(s1.at[c, pl.ds(0, 2 * (half - 1))], ss1.at[c])
        wait(r1.at[c, pl.ds(0, half)], ssf.at[c])
        wait(s2.at[c, pl.ds(0, half - 1)], ss2.at[c])
        wait(s3.at[pl.ds(0, gy - 1), c], ss3.at[c])
        return 0

    lax.fori_loop(0, planes, finish, 0)


def write_out(done, out, sems):
    size = done.shape[1] // (WRITES // 2)
    copies = []
    for i in range(WRITES):
        at = (i % 2, pl.ds(i // 2 * size, size))
        copies.append(pltpu.make_async_copy(done.at[at], out.at[at], sems.at[i]))
        copies[-1].start()
    for copy in copies:
        copy.wait()


def solution(mesh):
    gx, gy = mesh.shape["gx"], mesh.shape["gy"]

    def per_device(field):
        comp, depth, rows, cols = field.shape
        planes = comp * depth
        freqs = rows // gy
        ny = gy * cols
        groups = ny // LANES
        consts = tables(gx, gy, rows, cols, freqs)
        any_ = pl.BlockSpec(memory_space=pl.ANY)
        pieces = (rows // SUB) * (cols // LANES)
        assert pieces == gx
        vmem = lambda a: pltpu.VMEM(a.shape, a.dtype)
        dma = pltpu.SemaphoreType.DMA
        perm, turnx, xfirst, xlow, yhigh, ylow, turny = consts
        result = pl.pallas_call(
            functools.partial(kernel, gx, gy, planes),
            out_shape=pltpu.VMEM((2, planes, freqs, ny), F32),
            in_specs=[any_] * 8,
            out_specs=pl.BlockSpec(memory_space=pltpu.VMEM),
            scratch_shapes=[
                pltpu.VMEM((planes, rows, cols), F32),
                pltpu.VMEM((planes, gx, SUB, LANES), F32),
                pltpu.VMEM((planes, gx, 2, SUB, LANES), F32),
                pltpu.VMEM((planes, gx, 2, 2, SUB, LANES), F32),
                pltpu.VMEM((planes, gx // 2, 2, 2, SUB, LANES), F32),
                pltpu.VMEM((gy, planes, 2, freqs, cols), F32),
                pltpu.VMEM((gy, planes, 2, freqs, cols), F32),
                pltpu.VMEM((groups, freqs, 2 * LANES), F32),
                pltpu.VMEM(perm.shape[1:], perm.dtype),
                pltpu.VMEM((FAMILIES,) + turnx.shape[1:], turnx.dtype),
                vmem(xfirst),
                vmem(xlow),
                vmem(yhigh),
                vmem(ylow),
                vmem(turny),
                dma((planes,)),
                dma((6 + FAMILIES,)),
                *[dma((planes,))] * 8,
            ],
            compiler_params=pltpu.CompilerParams(
                collective_id=0, has_side_effects=True, vmem_limit_bytes=50 << 20
            ),
        )(field.reshape(planes, rows, cols), *[jnp.asarray(c) for c in consts])
        result = pltpu.with_memory_space_constraint(result, pltpu.VMEM)
        result = pl.pallas_call(
            write_out,
            out_shape=jax.ShapeDtypeStruct(result.shape, F32),
            in_specs=[pl.BlockSpec(memory_space=pltpu.VMEM)],
            out_specs=any_,
            scratch_shapes=[dma((WRITES,))],
            compiler_params=pltpu.CompilerParams(vmem_limit_bytes=8 << 20),
        )(result)
        return result.reshape(2, comp, depth, freqs, ny)

    return jax.shard_map(
        per_device,
        mesh=mesh,
        in_specs=(P(None, None, "gx", "gy"),),
        out_specs=P(None, None, None, ("gx", "gy"), None),
        check_vma=False,
    )
```

time: 129 us -> 122 us (0.946)
  local copies, waits for them, and re-layouts: 6.29 us -> 0 us
    unnamed x1 -> x0, local copies, waits for them, and re-layouts: 6.29 us -> none
    pallas_call x1 -> x2, Pallas kernels: 121 us -> 121 us  [the longest x1 118 us: per_device(): pl.pallas_call(functools.partial(kernel, gx, gy, planes), out_shape=pltpu...]
where the time goes in v3:
time: 122 us; the launch traced here: 121 us
  Pallas kernels  121 us (99%)
    pallas_call x1, Pallas kernels, per_device(): pl.pallas_call(functools.partial(kernel, gx, gy, planes), out_shape=pltpu...  118 us
    pallas_call x1, Pallas kernels, per_device(): pl.pallas_call(write_out, out_shape=jax.ShapeDtypeStruct(result.shape, F3...  2.74 us

profile of v3, /device:TPU:3, one launch (start us, length us, event | category | flops | bytes accessed | tf_op | source)
XLA Modules:
  0.0 121.0 jit_solution(17435172628491443382)
XLA Ops:
  0.0 118.3 %shard_map.82.done = f32[2,24,16,2048]{3,2,1,0:T(8,128)S(1)} custom-call(f32[24,64,512]{2,1,0:T(8,128)} %bitcast.2, bf16[4,512,512]{2,1,0:T(8,128)(2,1)} %constant.14.clone.perm_hbm, f32[8,32,2,8,128]{4,3,2,1,0:T(8,128)} %constant.15.clone.turnx_hbm, bf16[128,256]{1,0:T(8,128)(2,1)} %constant.16.clone.xfirst_hbm, bf16[128,128]{1,0:T(8,128)(2,1)} %constant.17.clone.xlow_hbm, ...), custom_call_target="tpu_custom_call" | custom-call | tf_op jit(solution)/shard_map/pallas_call | solution.py:442
  118.3 2.7 %shard_map.83 = f32[2,24,16,2048]{3,2,1,0:T(8,128)} custom-call(f32[2,24,16,2048]{3,2,1,0:T(8,128)S(1)} %shard_map.82.done), custom_call_target="tpu_custom_call" | custom-call | tf_op jit(solution)/shard_map/pallas_call | solution.py:472

commit v4 on v3

--- a/solution.py
+++ b/solution.py
@@ -18,10 +18,10 @@
 WRITES = 8
 PLACES = (2, 8, 4, 16)
 FAMILIES = len(PLACES)
-AHEAD = 6
-LAG_A = 4
-LAG_B = 7
-LAG_C = 9
+AHEAD = 9
+LAG_A = 6
+LAG_B = 11
+LAG_C = 15
 
 
 def bit_reverse(value, digits):
@@ -178,18 +178,31 @@
     groups = turny.shape[0]
     per = yhigh.shape[0]
     half = gx // 2
-
-    def bit_of(family):
-        place = PLACES[0]
-        for f in range(1, FAMILIES):
-            place = jnp.where(family == f, PLACES[f], place)
-        return place, code // place % 2
+    units = 2 * planes
+
+    def toggles(value, weights):
+        return [(1 - value // w % 2 * 2) * w for w in weights]
+
+    flip_me = toggles(me, [1 << i for i in range(gx.bit_length() - 1)])
+
+    def flipped(value, flips, mask):
+        for i, f in enumerate(flips):
+            if mask >> i & 1:
+                value = value + f
+        return value
 
     def piece(place):
         return code // (2 * place) * place + code % place
 
-    def device(index, place, bit):
-        return ungray(index // place * (2 * place) + bit * place + index % place)
+    def by_family(c, body):
+        for f, place in enumerate(PLACES):
+
+            @pl.when(lax.rem(c, FAMILIES) == f)
+            def _(place=place):
+                body(place)
+
+    def peers(place):
+        return [(k, ungray(k // place * (2 * place) + k % place)) for k in range(half)]
 
     def load(c):
         return pltpu.make_async_copy(field.at[c], raw.at[c], in_sem.at[c])
@@ -236,45 +249,40 @@
         pltpu.make_async_copy(ref, ref, sem).wait()
 
     def exchange_raw(c):
-        place, bit = bit_of(lax.rem(c, FAMILIES))
-        own = piece(place)
-        pltpu.make_async_copy(s1.at[c, pl.ds(2 * own, 2)], r1.at[c, me], rs1.at[c]).start()
-
-        def one(k, _):
-            i = lax.rem(own + k, half)
-            send(s1.at[c, pl.ds(2 * i, 2)], r1.at[c, me], ss1.at[c], rs1.at[c], (device(i, place, bit), my))
-            return 0
-
-        lax.fori_loop(1, half, one, 0)
+        def body(place):
+            own = piece(place)
+            flips = toggles(own, [1 << i for i in range(half.bit_length() - 1)])
+            pltpu.make_async_copy(s1.at[c, own], r1.at[c, me], rs1.at[c]).start()
+            for k, mask in peers(place)[1:]:
+                there = (flipped(me, flip_me, mask), my)
+                send(s1.at[c, flipped(own, flips, k)], r1.at[c, me], ss1, rs1.at[c], there)
+
+        by_family(c, body)
 
     def forward(c):
-        place, bit = bit_of(lax.rem(c, FAMILIES))
-        other = ungray(code + place - 2 * place * bit)
-
-        def one(i, _):
-            g = device(i, place, bit)
-            send(r1.at[c, g], r1.at[c, g], ssf.at[c], rsf.at[c], (other, my))
-            return 0
-
-        lax.fori_loop(0, half, one, 0)
+        def body(place):
+            other = (flipped(me, flip_me, ungray(place)), my)
+            for k, mask in peers(place):
+                g = flipped(me, flip_me, mask)
+                send(r1.at[c, g], r1.at[c, g], ssf, rsf.at[c], other)
+
+        by_family(c, body)
 
     def exchange_x(c):
-        place, bit = bit_of(lax.rem(c, FAMILIES))
-        own = piece(place)
-        pltpu.make_async_copy(s2.at[c, me], r2.at[c, own], rs2.at[c]).start()
-
-        def one(k, _):
-            t = device(lax.rem(own + k, half), place, bit)
-            send(s2.at[c, t], r2.at[c, own], ss2.at[c], rs2.at[c], (t, my))
-            return 0
-
-        lax.fori_loop(1, half, one, 0)
+        def body(place):
+            own = piece(place)
+            pltpu.make_async_copy(s2.at[c, me], r2.at[c, own], rs2.at[c]).start()
+            for k, mask in peers(place)[1:]:
+                there = flipped(me, flip_me, mask)
+                send(s2.at[c, there], r2.at[c, own], ss2, rs2.at[c], (there, my))
+
+        by_family(c, body)
 
     def exchange_y(c):
         pltpu.make_async_copy(s3.at[my, c], r3.at[my, c], rs3.at[c]).start()
         for j in range(1, gy):
             t = lax.rem(my + j, gy)
-            send(s3.at[t, c], r3.at[my, c], ss3.at[c], rs3.at[c], (me, t))
+            send(s3.at[t, c], r3.at[my, c], ss3, rs3.at[c], (me, t))
 
     def permute(c):
         load(c).wait()
@@ -283,38 +291,34 @@
         moved = both[:rows] + both[rows:]
         for t in range(tiles):
             for w in range(wide):
-                s1[c, t * wide + w] = moved[t * SUB : (t + 1) * SUB, w * LANES : (w + 1) * LANES]
+                s1[2 * c + w % 2, (t * wide + w) // 2] = moved[t * SUB : (t + 1) * SUB, w * LANES : (w + 1) * LANES]
 
     def over_gx(c):
         family = lax.rem(c, FAMILIES)
 
-        def one(w, _):
-            got = real_fft([r1[c, g, w] for g in range(gx)])
-            for i in range(gx):
-                r = bit_reverse(i, gx.bit_length() - 1)
-                re, im = got[r] if 2 * r <= gx else conj(got[gx - r])
-                if r == 0:
-                    s2[c, i, w, 0] = re
-                    s2[c, i, w, 1] = jnp.zeros_like(re)
-                    continue
-                tr, ti = turnx[family, i, 0], turnx[family, i, 1]
-                if im is None:
-                    s2[c, i, w, 0] = re * tr
-                    s2[c, i, w, 1] = re * ti
-                else:
-                    s2[c, i, w, 0] = re * tr - im * ti
-                    s2[c, i, w, 1] = re * ti + im * tr
-            return 0
-
-        lax.fori_loop(0, 2, one, 0)
+        got = real_fft([r1[c, g] for g in range(gx)])
+        for i in range(gx):
+            r = bit_reverse(i, gx.bit_length() - 1)
+            re, im = got[r] if 2 * r <= gx else conj(got[gx - r])
+            if r == 0:
+                s2[c, i, 0] = re
+                s2[c, i, 1] = jnp.zeros_like(re)
+                continue
+            tr, ti = turnx[family, i, 0], turnx[family, i, 1]
+            if im is None:
+                s2[c, i, 0] = re * tr
+                s2[c, i, 1] = re * ti
+            else:
+                s2[c, i, 0] = re * tr - im * ti
+                s2[c, i, 1] = re * ti + im * tr
 
     def over_m(c):
         value = jnp.concatenate(
             [
                 jnp.concatenate(
-                    [r2[c, (t * wide + w) // 2, w % 2, part] for part in range(2) for t in range(tiles)], axis=0
+                    [r2[c, t * wide // 2 + w, part] for part in range(2) for t in range(tiles)], axis=0
                 )
-                for w in range(wide)
+                for w in range(wide // 2)
             ],
             axis=1,
         )
@@ -333,7 +337,8 @@
             for w in range(wide):
                 halves = []
                 for part in range(2):
-                    got = [r3[s, c, part, :, w * LANES : (w + 1) * LANES] for s in range(gy)]
+                    at = slice(w // 2 * LANES, (w // 2 + 1) * LANES)
+                    got = [r3[s, 2 * c + w % 2, part, :, at] for s in range(gy)]
                     merged = got[-q % per]
                     for g in range(1, per):
                         merged = jnp.where(group == g, got[(g - q) % per], merged)
@@ -360,7 +365,10 @@
                 out[1, c, at, k * LANES : (k + 1) * LANES] = im
 
     def enter(c, _):
-        permute(c)
+        @pl.when(lax.rem(c, 2) == 0)
+        def _():
+            permute(lax.div(c, 2))
+
         exchange_raw(c)
         return 0
 
@@ -369,23 +377,23 @@
         copy.wait()
 
     def turn_step(i, _):
-        @pl.when(i < planes - AHEAD)
+        @pl.when(i < units - AHEAD)
         def _():
             enter(i + AHEAD, 0)
 
-        @pl.when(i < planes)
+        @pl.when(i < units)
         def _():
             wait(r1.at[i, pl.ds(0, half)], rs1.at[i])
             forward(i)
 
-        @pl.when(jnp.logical_and(i >= LAG_A, i < planes + LAG_A))
+        @pl.when(jnp.logical_and(i >= LAG_A, i < units + LAG_A))
         def _():
             c = i - LAG_A
             wait(r1.at[c, pl.ds(0, half)], rsf.at[c])
             over_gx(c)
             exchange_x(c)
 
-        @pl.when(jnp.logical_and(i >= LAG_B, i < planes + LAG_B))
+        @pl.when(jnp.logical_and(i >= LAG_B, i < units + LAG_B))
         def _():
             c = i - LAG_B
             wait(r2.at[c], rs2.at[c])
@@ -396,20 +404,19 @@
         def _():
             c = i - LAG_C
             wait(r3.at[:, c], rs3.at[c])
-            over_y(c)
+
+            @pl.when(lax.rem(c, 2) == 1)
+            def _():
+                over_y(lax.div(c, 2))
 
         return 0
 
-    lax.fori_loop(0, planes + LAG_C, turn_step, 0)
-
-    def finish(c, _):
-        wait(s1.at[c, pl.ds(0, 2 * (half - 1))], ss1.at[c])
-        wait(r1.at[c, pl.ds(0, half)], ssf.at[c])
-        wait(s2.at[c, pl.ds(0, half - 1)], ss2.at[c])
-        wait(s3.at[pl.ds(0, gy - 1), c], ss3.at[c])
-        return 0
-
-    lax.fori_loop(0, planes, finish, 0)
+    lax.fori_loop(0, units + LAG_C, turn_step, 0)
+
+    wait(s1.at[:, pl.ds(0, half - 1)], ss1)
+    wait(r1.at[:, pl.ds(0, half)], ssf)
+    wait(s2.at[:, pl.ds(0, half - 1)], ss2)
+    wait(s3.at[pl.ds(0, gy - 1)], ss3)
 
 
 def write_out(done, out, sems):
@@ -429,6 +436,7 @@
     def per_device(field):
         comp, depth, rows, cols = field.shape
         planes = comp * depth
+        units = 2 * planes
         freqs = rows // gy
         ny = gy * cols
         groups = ny // LANES
@@ -446,12 +454,12 @@
             out_specs=pl.BlockSpec(memory_space=pltpu.VMEM),
             scratch_shapes=[
                 pltpu.VMEM((planes, rows, cols), F32),
-                pltpu.VMEM((planes, gx, SUB, LANES), F32),
-                pltpu.VMEM((planes, gx, 2, SUB, LANES), F32),
-                pltpu.VMEM((planes, gx, 2, 2, SUB, LANES), F32),
-                pltpu.VMEM((planes, gx // 2, 2, 2, SUB, LANES), F32),
-                pltpu.VMEM((gy, planes, 2, freqs, cols), F32),
-                pltpu.VMEM((gy, planes, 2, freqs, cols), F32),
+                pltpu.VMEM((units, gx // 2, SUB, LANES), F32),
+                pltpu.VMEM((units, gx, SUB, LANES), F32),
+                pltpu.VMEM((units, gx, 2, SUB, LANES), F32),
+                pltpu.VMEM((units, gx // 2, 2, SUB, LANES), F32),
+                pltpu.VMEM((gy, units, 2, freqs, cols // 2), F32),
+                pltpu.VMEM((gy, units, 2, freqs, cols // 2), F32),
                 pltpu.VMEM((groups, freqs, 2 * LANES), F32),
                 pltpu.VMEM(perm.shape[1:], perm.dtype),
                 pltpu.VMEM((FAMILIES,) + turnx.shape[1:], turnx.dtype),
@@ -462,7 +470,7 @@
                 vmem(turny),
                 dma((planes,)),
                 dma((6 + FAMILIES,)),
-                *[dma((planes,))] * 8,
+                *[pltpu.SemaphoreType.DMA, dma((units,))] * 4,
             ],
             compiler_params=pltpu.CompilerParams(
                 collective_id=0, has_side_effects=True, vmem_limit_bytes=50 << 20

time: 122 us -> 119 us (0.975); the launches traced: 121 us -> 117 us
  Pallas kernels: 121 us -> 117 us
    pallas_call x1, Pallas kernels: 118 us -> 114 us  [per_device(): pl.pallas_call(functools.partial(kernel, gx, gy, planes), out_shape=pltpu...]
where the time goes in v4:
time: 119 us; the launch traced here: 117 us
  Pallas kernels  117 us (98%)
    pallas_call x1, Pallas kernels, per_device(): pl.pallas_call(functools.partial(kernel, gx, gy, planes), out_shape=pltpu...  114 us
    pallas_call x1, Pallas kernels, per_device(): pl.pallas_call(write_out, out_shape=jax.ShapeDtypeStruct(result.shape, F3...  2.74 us

profile of v4, /device:TPU:3, one launch (start us, length us, event | category | flops | bytes accessed | tf_op | source)
XLA Modules:
  0.0 116.6 jit_solution(11695639270846060671)
XLA Ops:
  0.0 113.8 %shard_map.82.done = f32[2,24,16,2048]{3,2,1,0:T(8,128)S(1)} custom-call(f32[24,64,512]{2,1,0:T(8,128)} %bitcast.2, bf16[4,512,512]{2,1,0:T(8,128)(2,1)} %constant.14.clone.perm_hbm, f32[8,32,2,8,128]{4,3,2,1,0:T(8,128)} %constant.15.clone.turnx_hbm, bf16[128,256]{1,0:T(8,128)(2,1)} %constant.16.clone.xfirst_hbm, bf16[128,128]{1,0:T(8,128)(2,1)} %constant.17.clone.xlow_hbm, ...), custom_call_target="tpu_custom_call" | custom-call | tf_op jit(solution)/shard_map/pallas_call | solution.py:450
  113.9 2.7 %shard_map.83 = f32[2,24,16,2048]{3,2,1,0:T(8,128)} custom-call(f32[2,24,16,2048]{3,2,1,0:T(8,128)S(1)} %shard_map.82.done), custom_call_target="tpu_custom_call" | custom-call | tf_op jit(solution)/shard_map/pallas_call | solution.py:480

commit v5 on v4

--- a/solution.py
+++ b/solution.py
@@ -18,10 +18,10 @@
 WRITES = 8
 PLACES = (2, 8, 4, 16)
 FAMILIES = len(PLACES)
-AHEAD = 9
-LAG_A = 6
-LAG_B = 11
-LAG_C = 15
+AHEAD = 12
+LAG_A = 8
+LAG_B = 13
+LAG_C = 17
 
 
 def bit_reverse(value, digits):

time: 119 us -> 118 us (level)
  no operation moved by 1% of the time
where the time goes in v5:
time: 118 us; the launch traced here: 116 us
  Pallas kernels  116 us (98%)
    pallas_call x1, Pallas kernels, per_device(): pl.pallas_call(functools.partial(kernel, gx, gy, planes), out_shape=pltpu...  113 us
    pallas_call x1, Pallas kernels, per_device(): pl.pallas_call(write_out, out_shape=jax.ShapeDtypeStruct(result.shape, F3...  2.74 us

profile of v5, /device:TPU:3, one launch (start us, length us, event | category | flops | bytes accessed | tf_op | source)
XLA Modules:
  0.0 116.2 jit_solution(15254757540931031924)
XLA Ops:
  0.0 113.4 %shard_map.82.done = f32[2,24,16,2048]{3,2,1,0:T(8,128)S(1)} custom-call(f32[24,64,512]{2,1,0:T(8,128)} %bitcast.2, bf16[4,512,512]{2,1,0:T(8,128)(2,1)} %constant.14.clone.perm_hbm, f32[8,32,2,8,128]{4,3,2,1,0:T(8,128)} %constant.15.clone.turnx_hbm, bf16[128,256]{1,0:T(8,128)(2,1)} %constant.16.clone.xfirst_hbm, bf16[128,128]{1,0:T(8,128)(2,1)} %constant.17.clone.xlow_hbm, ...), custom_call_target="tpu_custom_call" | custom-call | tf_op jit(solution)/shard_map/pallas_call | solution.py:450
  113.5 2.7 %shard_map.83 = f32[2,24,16,2048]{3,2,1,0:T(8,128)} custom-call(f32[2,24,16,2048]{3,2,1,0:T(8,128)S(1)} %shard_map.82.done), custom_call_target="tpu_custom_call" | custom-call | tf_op jit(solution)/shard_map/pallas_call | solution.py:480
